TPU v7x, 32 devices: a whole 2x2x4 slice. The times are simulated.
32 devices in a mesh: expert: 4 (over z), tensor: 8 (over y, x, core).
Axes of the slice: x: 2, y: 2, z: 4, core: 2. Of those that a mesh axis runs over, the one named last changes fastest.
Arguments:
- activations: bfloat16 [3072, 512], P('tensor', 'expert'), may hold values from -6 to 6
- cotangent: bfloat16 [3072, 512], P('tensor', 'expert'), may hold values from -4 to 4
- route_ids: int32 [512, 2], P('expert'), may hold values from 0 to 3, all different within a row; in each aligned block of 128 rows (0 to 127, 128 to 255, ...) at most 80 rows name the same one
- gate_probs: float32 [512, 2], P('expert'), may hold values from 0.2 to 0.8
- gate_weight: bfloat16 [4, 3072, 16384], P('expert', None, 'tensor'), may hold values from -0.15625 to 0.15625
- up_weight: bfloat16 [4, 3072, 16384], P('expert', None, 'tensor'), may hold values from -0.15625 to 0.15625
- down_weight: bfloat16 [4, 16384, 3072], P('expert', 'tensor'), may hold values from -0.046875 to 0.046875
Outputs:
- grad_input: bfloat16 [3072, 512], P('tensor', 'expert')
- score_grad: float32 [512, 2], P('expert')
Inputs may be any that keep to these rules, and one draw needn't show every extreme that they name: `route_ids`: each token names 2 different experts. Among the 128 tokens of one index of the expert axis no expert is named more than 80 times, and in every draw some such block names one expert exactly 80 times.
All inputs are finite; a program needn't handle non-finite values.
Results may differ from a plain program's by a relative error of at most 0.008.
Values may be sent and summed in bfloat16 or wider, within the bound.
A program may use at most 128 MiB of HBM per device.

v0:
```python
import jax
import jax.numpy as jnp
from jax import lax
from jax.sharding import PartitionSpec as P

EXTRA_ROWS = 16


def slot_numbers(route_ids, expert_count, capacity):
    token_count = route_ids.shape[0]
    onehot = route_ids[:, :, None] == jnp.arange(expert_count, dtype=jnp.int32)[None, None, :]
    named = jnp.sum(onehot.astype(jnp.float32), axis=1).astype(jnp.bfloat16)
    order = jnp.arange(token_count, dtype=jnp.int32)
    before = (order[None, :] < order[:, None]).astype(jnp.bfloat16)
    earlier = jnp.dot(before, named, preferred_element_type=jnp.float32)
    position = jnp.sum(jnp.where(onehot, earlier[:, None, :], 0.0), axis=2).astype(jnp.int32)
    return route_ids * capacity + position


def swiglu_backward(gate_sum, up_sum, hidden_grad):
    sigma = jax.nn.sigmoid(gate_sum)
    silu_value = gate_sum * sigma
    grad_up = (hidden_grad * silu_value).astype(jnp.bfloat16)
    grad_gate = (hidden_grad * up_sum * sigma * (1.0 + gate_sum * (1.0 - sigma))).astype(
        jnp.bfloat16
    )
    score_rows = jnp.sum(silu_value * up_sum * hidden_grad, axis=1)
    return (grad_gate, grad_up, score_rows)


def body(activations, cotangent, route_ids, gate_probs, gate_weight, up_weight, down_weight):
    expert_count = lax.axis_size("expert")
    tokens_here = route_ids.shape[0]
    capacity = min(tokens_here, 5 * tokens_here // (2 * expert_count))
    slot_total = expert_count * capacity
    destination = slot_numbers(route_ids, expert_count, capacity)
    slot_range = jnp.arange(slot_total, dtype=jnp.int32)
    matches = destination[:, :, None] == slot_range[None, None, :]
    placing = jnp.sum(matches.astype(jnp.float32), axis=1).astype(jnp.bfloat16)
    weighting = jnp.sum(jnp.where(matches, gate_probs[:, :, None], jnp.float32(0.0)), axis=1)
    gate_local = gate_weight[0]
    up_local = up_weight[0]
    down_local = down_weight[0]
    first_dims = (((0,), (0,)), ((), ()))
    down_dims = (((0,), (1,)), ((), ()))
    hidden_dims = (((1,), (1,)), ((), ()))
    features_here = activations.shape[0]
    send_in = jnp.dot(activations, placing, preferred_element_type=jnp.float32).astype(jnp.bfloat16)
    send_grad = jnp.dot(cotangent, placing, preferred_element_type=jnp.float32).astype(jnp.bfloat16)
    recv_in, recv_grad = (
        lax.all_to_all(send_in, "expert", split_axis=1, concat_axis=1, tiled=True),
        lax.all_to_all(send_grad, "expert", split_axis=1, concat_axis=1, tiled=True),
    )
    feature_piece = lax.all_gather(recv_in, "tensor", axis=0, tiled=True)
    grad_piece = lax.all_gather(recv_grad, "tensor", axis=0, tiled=True)
    gate_rows = gate_local
    up_rows = up_local
    gate_sum = lax.dot_general(
        feature_piece, gate_rows, first_dims, preferred_element_type=jnp.float32
    )
    up_sum = lax.dot_general(feature_piece, up_rows, first_dims, preferred_element_type=jnp.float32)
    hidden_grad = lax.dot_general(
        grad_piece, down_local, down_dims, preferred_element_type=jnp.float32
    )
    gate_sum, up_sum, hidden_grad = (gate_sum, up_sum, hidden_grad)
    grad_gate, grad_up, score_rows = swiglu_backward(gate_sum, up_sum, hidden_grad)
    gate_rows = gate_local
    up_rows = up_local
    term = lax.dot_general(gate_rows, grad_gate, hidden_dims, preferred_element_type=jnp.float32)
    term = term + lax.dot_general(up_rows, grad_up, hidden_dims, preferred_element_type=jnp.float32)
    tensor_count = lax.axis_size("tensor")
    score_high = score_rows.astype(jnp.bfloat16)
    score_low = (score_rows - score_high.astype(jnp.float32)).astype(jnp.bfloat16)
    extra = jnp.concatenate(
        [
            score_high[None, :],
            score_low[None, :],
            jnp.zeros((EXTRA_ROWS - 2, slot_total), jnp.bfloat16),
        ],
        axis=0,
    )
    blocks = term.astype(jnp.bfloat16).reshape(tensor_count, features_here, slot_total)
    extra = jnp.broadcast_to(extra[None], (tensor_count, EXTRA_ROWS, slot_total))
    parts = lax.all_to_all(
        jnp.concatenate([blocks, extra], axis=1), "tensor", split_axis=0, concat_axis=0, tiled=True
    ).astype(jnp.float32)
    totals = jnp.sum(parts, axis=0)
    score = (
        totals[features_here : features_here + 1] + totals[features_here + 1 : features_here + 2]
    )
    score_high = score.astype(jnp.bfloat16)
    score_low = (score - score_high.astype(jnp.float32)).astype(jnp.bfloat16)
    summed = jnp.concatenate(
        [
            totals[:features_here].astype(jnp.bfloat16),
            score_high,
            score_low,
            jnp.zeros((EXTRA_ROWS - 2, slot_total), jnp.bfloat16),
        ],
        axis=0,
    )
    back = lax.all_to_all(summed, "expert", split_axis=1, concat_axis=1, tiled=True)
    back = back.astype(jnp.float32)
    back_terms = back[:features_here]
    back_scores = (
        back[features_here : features_here + 1] + back[features_here + 1 : features_here + 2]
    )
    grad_local = jnp.dot(
        back_terms, weighting.T, precision=lax.Precision.HIGHEST, preferred_element_type=jnp.float32
    )
    score_grad = jnp.sum(
        jnp.where(matches, back_scores[0][None, None, :], jnp.float32(0.0)), axis=2
    )
    grad_input = grad_local.astype(jnp.bfloat16)
    return (grad_input, score_grad)


def solution(mesh):
    in_specs = (
        P("tensor", "expert"),
        P("tensor", "expert"),
        P("expert", None),
        P("expert", None),
        P("expert", None, "tensor"),
        P("expert", None, "tensor"),
        P("expert", "tensor", None),
    )
    out_specs = (P("tensor", "expert"), P("expert", None))
    return jax.shard_map(body, mesh=mesh, in_specs=in_specs, out_specs=out_specs, check_vma=False)
```

profile of v0, /device:TPU:0, one launch (start us, length us, event | category | flops | bytes accessed | tf_op | source)
XLA Modules:
  0.0 178.5 jit_solution(15263084820237573660)
XLA Ops:
  7.2 0.0 copy-start
  7.2 0.0 all-gather.5.cloned.1.call-start
  7.2 0.7 convert_reduce_fusion.2
  7.9 0.1 fusion.23
  8.1 0.7 select_reduce_fusion.2
  8.8 0.7 convert_add_fusion
  9.5 0.0 copy-done
  9.5 0.2 convolution_convert_fusion
  9.8 14.7 %all_to_all.38 = bf16[384,4,80]{0,2,1:T(8,128)(2,1)} all-to-all(bf16[384,4,80]{0,2,1:T(8,128)(2,1)S(1)} %bitcast.50), channel_id=1, replica_groups=mesh['expert'=4,'tensor'=8] {'expert'}, dimensions={1} | all-to-all | bytes 491520 | tf_op jit(solution)/shard_map/all_to_all | solution.py:51
  24.5 0.0 all-gather.5.cloned.1.call-update
  24.5 0.0 all-gather.3.cloned.1.call-start
  24.6 1.1 convolution_convert_fusion.1
  25.7 10.7 %all_to_all.39 = bf16[384,4,80]{0,2,1:T(8,128)(2,1)} all-to-all(bf16[384,4,80]{0,2,1:T(8,128)(2,1)S(1)} %bitcast.49), channel_id=1, replica_groups=mesh['expert'=4,'tensor'=8] {'expert'}, dimensions={1} | all-to-all | bytes 491520 | tf_op jit(solution)/shard_map/all_to_all | solution.py:52
  36.5 0.0 all-gather.3.cloned.1.call-update
  36.5 14.9 %all-gather.5.cloned.1.call-done = bf16[3072,320]{0,1:T(8,128)(2,1)} async-done(((bf16[384,320]{0,1:T(8,128)(2,1)}), bf16[3072,320]{0,1:T(8,128)(2,1)}) %all-gather.5.cloned.1.call-update) | async-done | bytes 1966096 | tf_op jit(solution)/shard_map/all_gather | solution.py:54
  51.4 0.0 copy-start.3
  51.4 9.4 %fusion.2 = f32[320,2048]{1,0:T(8,128)S(1)} fusion(bf16[3072,320]{0,1:T(8,128)(2,1)} %all-gather.5.cloned.1.call-done, bf16[1,3072,2048]{2,1,0:T(8,128)(2,1)} %param.11), kind=kOutput, calls=%fused_computation.2 | convolution fusion | flops 4026531840 | bytes 17170432 | tf_op jit(solution)/shard_map/dot_general | solution.py:58
  60.8 0.0 copy-done.3
  60.8 8.8 %fusion.6 = f32[320,2048]{1,0:T(8,128)} fusion(bf16[3072,320]{0,1:T(8,128)(2,1)S(1)} %copy-done.3, bf16[1,3072,2048]{2,1,0:T(8,128)(2,1)} %param.12), kind=kOutput, calls=%fused_computation.6 | convolution fusion | flops 4026531840 | bytes 17170432 | tf_op jit(solution)/shard_map/dot_general | solution.py:61
  69.6 11.3 %all-gather.3.cloned.1.call-done = bf16[3072,320]{0,1:T(8,128)(2,1)} async-done(((bf16[384,320]{0,1:T(8,128)(2,1)}), bf16[3072,320]{0,1:T(8,128)(2,1)}) %all-gather.3.cloned.1.call-update) | async-done | bytes 1966096 | tf_op jit(solution)/shard_map/all_gather | solution.py:55
  80.9 12.0 %multiply_reduce_fusion = (f32[320]{0:T(512)S(1)}, f32[320,2048]{1,0:T(8,128)}) fusion(f32[320,2048]{1,0:T(8,128)} %fusion.6, f32[320,2048]{1,0:T(8,128)S(1)} %fusion.2, bf16[3072,320]{0,1:T(8,128)(2,1)} %all-gather.3.cloned.1.call-done, bf16[1,2048,3072]{2,1,0:T(8,128)(2,1)} %param.13), kind=kOutput, calls=%fused_computation.14 | convolution fusion | flops 4031119104 | bytes 22414592 | tf_op jit(solution)/shard_map/dot_general | solution.py:62
  93.0 12.8 %fusion = f32[320,3072]{1,0:T(8,128)} fusion(bf16[1,3072,2048]{2,1,0:T(8,128)(2,1)} %param.11, f32[320,2048]{1,0:T(8,128)S(1)} %fusion.2, f32[320,2048]{1,0:T(8,128)} %get-tuple-element.7, f32[320,2048]{1,0:T(8,128)} %fusion.6), kind=kOutput, calls=%fused_computation | convolution fusion | flops 4033085440 | bytes 24379392 | tf_op jit(solution)/shard_map/dot_general | solution.py:69
  105.8 12.1 %fusion.16 = bf16[3072,320]{0,1:T(8,128)(2,1)} fusion(f32[320,3072]{1,0:T(8,128)} %fusion, bf16[1,3072,2048]{2,1,0:T(8,128)(2,1)} %param.12, f32[320,2048]{1,0:T(8,128)} %get-tuple-element.7, f32[320,2048]{1,0:T(8,128)S(1)} %fusion.2), kind=kOutput, calls=%fused_computation.13 | convolution fusion | flops 4032430080 | bytes 23724032 | tf_op jit(solution)/shard_map/dot_general | solution.py:70
  117.9 2.9 %copy.40 = bf16[3072,320]{1,0:T(8,128)(2,1)S(1)} copy(bf16[3072,320]{0,1:T(8,128)(2,1)} %fusion.16) | data formatting | bytes 3932160 | tf_op jit(solution)/shard_map/reshape | solution.py:82
  120.9 0.3 pad_maximum_fusion
  121.1 33.0 %all_to_all.40 = bf16[8,400,320]{2,1,0:T(8,128)(2,1)S(1)} all-to-all(bf16[8,400,320]{2,1,0:T(8,128)(2,1)S(1)} %pad_maximum_fusion), channel_id=1, replica_groups=mesh['expert'=4,'tensor'=8] {'tensor'}, dimensions={0} | all-to-all | bytes 4096000 | tf_op jit(solution)/shard_map/all_to_all | solution.py:84
  154.1 0.0 copy-start.1
  154.1 0.4 convert_reduce_fusion
  154.5 0.0 copy-start.2
  154.7 0.2 copy.39
  154.8 14.5 %all_to_all.41 = bf16[400,4,80]{0,2,1:T(8,128)(2,1)S(1)} all-to-all(bf16[400,4,80]{0,2,1:T(8,128)(2,1)S(1)} %bitcast.45), channel_id=1, replica_groups=mesh['expert'=4,'tensor'=8] {'expert'}, dimensions={1} | all-to-all | bytes 512000 | tf_op jit(solution)/shard_map/all_to_all | solution.py:102
  169.3 0.1 convert_element_type.115
  169.4 0.2 fusion.22
  169.6 0.1 broadcast_in_dim.57
  169.7 0.0 copy-done.2
  169.7 0.7 select_reduce_fusion
  170.4 1.2 convolution_convert_fusion.2
  171.6 0.0 copy-done.1
  (10 shorter events, 0.2 us)
Async XLA Ops:
  7.2 2.3 %copy-start = (bf16[384,128]{1,0:T(8,128)(2,1)S(1)}, bf16[384,128]{1,0:T(8,128)(2,1)}, u32[]{:S(2)}) copy-start(bf16[384,128]{1,0:T(8,128)(2,1)} %param.7) | copy-start | bytes 294916
  7.2 44.2 %all-gather.5.cloned.1.call-start = ((), (), s32[]{:S(2)}) async-start(), calls=%async_computation.5 | async-start | bytes 2211840 | tf_op jit(solution)/shard_map/all_gather | solution.py:54
  24.5 56.4 %all-gather.3.cloned.1.call-start = ((), (), s32[]{:S(2)}) async-start(), calls=%async_computation.4 | async-start | bytes 2211840 | tf_op jit(solution)/shard_map/all_gather | solution.py:55
  51.4 9.4 %copy-start.3 = (bf16[3072,320]{0,1:T(8,128)(2,1)S(1)}, bf16[3072,320]{0,1:T(8,128)(2,1)}, u32[]{:S(2)}) copy-start(bf16[3072,320]{0,1:T(8,128)(2,1)} %all-gather.5.cloned.1.call-done) | copy-start | bytes 5898244
  154.1 17.5 %copy-start.1 = (bf16[384,128]{1,0:T(8,128)(2,1)S(1)}, bf16[384,128]{1,0:T(8,128)(2,1)}, u32[]{:S(2)}) copy-start(bf16[384,128]{1,0:T(8,128)(2,1)} %param.7) | copy-start | bytes 294916
  154.5 15.2 %copy-start.2 = (f32[128,2]{0,1:T(2,128)S(1)}, f32[128,2]{0,1:T(2,128)}, u32[]{:S(2)}) copy-start(f32[128,2]{0,1:T(2,128)} %param.10) | copy-start | bytes 3076
Sparse Core Ops, SparseCore 0:
  24.7 26.7 all-gather.4
  53.3 27.6 all-gather.2
where the time goes:
time: 179 us; the launch traced here: 178 us
  blocking collectives  73 us (41%)
  matrix products  57.8 us (32%)
  waiting for transfers between devices  26.3 us (15%)
  between operations  14.2 us (8%)
  other arithmetic  3.87 us (2%)
  local copies, waits for them, and re-layouts  3.26 us (2%)
    all_to_all x1, blocking collectives, body(): lax.all_to_all(jnp.concatenate([blocks, extra], axis=1), 'tensor', split_...  33 us
    all_gather x1, waiting for transfers between devices, body(): feature_piece = lax.all_gather(recv_in, 'tensor', axis=0, tiled=True)  14.9 us
    all_to_all x1, blocking collectives, body(): lax.all_to_all(send_in, 'expert', split_axis=1, concat_axis=1, tiled=True)  14.7 us
    all_to_all x1, blocking collectives, body(): lax.all_to_all(summed, 'expert', split_axis=1, concat_axis=1, tiled=True)  14.5 us
    dot_general x1, matrix products, body(): lax.dot_general(gate_rows, grad_gate, hidden_dims, preferred_element_type...  12.8 us
    dot_general x1, matrix products, body(): lax.dot_general(up_rows, grad_up, hidden_dims, preferred_element_type=jnp...  12.1 us
    dot_general x1, matrix products, body(): lax.dot_general(grad_piece, down_local, down_dims, preferred_element_type...  12 us
    all_gather x1, waiting for transfers between devices, body(): grad_piece = lax.all_gather(recv_grad, 'tensor', axis=0, tiled=True)  11.3 us
  transfers between devices with their start and end apart: 2, of which 2 were waited for; matrix products, arithmetic and copies ran while one was open for 11% of the time, Pallas kernels for 0%

commit v1 on v0

--- a/solution.py
+++ b/solution.py
@@ -51,8 +51,11 @@
         lax.all_to_all(send_in, "expert", split_axis=1, concat_axis=1, tiled=True),
         lax.all_to_all(send_grad, "expert", split_axis=1, concat_axis=1, tiled=True),
     )
-    feature_piece = lax.all_gather(recv_in, "tensor", axis=0, tiled=True)
-    grad_piece = lax.all_gather(recv_grad, "tensor", axis=0, tiled=True)
+    feature_piece, grad_piece = jnp.split(
+        lax.all_gather(jnp.concatenate([recv_in, recv_grad], axis=1), "tensor", axis=0, tiled=True),
+        [recv_in.shape[1]],
+        axis=1,
+    )
     gate_rows = gate_local
     up_rows = up_local
     gate_sum = lax.dot_general(

time: 179 us -> 188 us (1.050)
  waiting for transfers between devices: 26.3 us -> 43 us
  blocking collectives: 73 us -> 57.8 us
  starting transfers between devices: 0.08 us -> 6.32 us
    all_to_all x1 -> x0, blocking collectives: 14.7 us -> none  [body(): lax.all_to_all(send_in, 'expert', split_axis=1, concat_axis=1, tiled=True)]
    all_gather x2 -> x1, waiting for transfers between devices: 26.3 us -> 35.5 us  [body(): lax.all_gather(jnp.concatenate([recv_in, recv_grad], axis=1), 'tensor', a...]
    all_to_all x0 -> x1, waiting for transfers between devices: none -> 7.43 us  [body(): lax.all_to_all(send_in, 'expert', split_axis=1, concat_axis=1, tiled=True)]
    all_to_all x0 -> x1, starting transfers between devices: none -> 6.31 us  [body(): lax.all_to_all(send_in, 'expert', split_axis=1, concat_axis=1, tiled=True)]
  transfers between devices with their start and end apart: 2 -> 2, of which waited for: 2 -> 2; matrix products, arithmetic and copies ran while one was open for 11% -> 1% of each run, Pallas kernels for 0% -> 0%
where the time goes in v1:
time: 188 us; the launch traced here: 187 us
  matrix products  58 us (31%)
  blocking collectives  57.8 us (31%)
  waiting for transfers between devices  43 us (23%)
  between operations  14.2 us (8%)
  starting transfers between devices  6.32 us (3%)
  other arithmetic  4.73 us (3%)
  local copies, waits for them, and re-layouts  3.26 us (2%)
    all_gather x1, waiting for transfers between devices, body(): lax.all_gather(jnp.concatenate([recv_in, recv_grad], axis=1), 'tensor', a...  35.5 us
    all_to_all x1, blocking collectives, body(): lax.all_to_all(jnp.concatenate([blocks, extra], axis=1), 'tensor', split_...  33 us
    all_to_all x1, blocking collectives, body(): lax.all_to_all(summed, 'expert', split_axis=1, concat_axis=1, tiled=True)  14.5 us
    dot_general x1, matrix products, body(): lax.dot_general(gate_rows, grad_gate, hidden_dims, preferred_element_type...  12.7 us
    dot_general x1, matrix products, body(): lax.dot_general(up_rows, grad_up, hidden_dims, preferred_element_type=jnp...  12.1 us
    dot_general x1, matrix products, body(): lax.dot_general(grad_piece, down_local, down_dims, preferred_element_type...  11.6 us
    all_to_all x1, blocking collectives, body(): lax.all_to_all(send_grad, 'expert', split_axis=1, concat_axis=1, tiled=True)  10.3 us
    dot_general x1, matrix products, body(): lax.dot_general(feature_piece, gate_rows, first_dims, preferred_element_t...  9.42 us
  transfers between devices with their start and end apart: 2, of which 2 were waited for; matrix products, arithmetic and copies ran while one was open for 1% of the time, Pallas kernels for 0%

profile of v1, /device:TPU:0, one launch (start us, length us, event | category | flops | bytes accessed | tf_op | source)
XLA Modules:
  0.0 187.2 jit_solution(7957560003654607083)
XLA Ops:
  7.2 0.0 copy-start
  7.2 0.7 convert_reduce_fusion.2
  7.9 0.1 fusion.26
  8.0 0.7 select_reduce_fusion.2
  8.8 0.7 convert_add_fusion
  9.5 0.0 copy-done
  9.5 0.9 convolution_convert_fusion.1
  10.4 6.3 %all-to-all-start = ((bf16[384,4,80]{0,2,1:T(8,128)(2,1)}), bf16[384,4,80]{0,2,1:T(8,128)(2,1)S(1)}, u32[]{:S(2)}, u32[]{:S(2)}) async-start(bf16[384,4,80]{0,2,1:T(8,128)(2,1)} %bitcast.1), calls=%async_computation | async-start | bytes 491520 | tf_op jit(solution)/shard_map/all_to_all | solution.py:51
  16.7 0.0 all-gather.2.cloned.1.call-start
  16.7 1.1 convolution_convert_fusion
  17.9 7.4 %all-to-all-done = bf16[384,4,80]{0,2,1:T(8,128)(2,1)S(1)} async-done(((bf16[384,4,80]{0,2,1:T(8,128)(2,1)}), bf16[384,4,80]{0,2,1:T(8,128)(2,1)S(1)}, u32[]{:S(2)}, u32[]{:S(2)}) %all-to-all-start) | async-done | bytes 245792 | tf_op jit(solution)/shard_map/all_to_all | solution.py:51
  25.3 10.3 %all_to_all.38 = bf16[384,4,80]{0,2,1:T(8,128)(2,1)S(1)} all-to-all(bf16[384,4,80]{0,2,1:T(8,128)(2,1)S(1)} %bitcast.43), channel_id=1, replica_groups=mesh['expert'=4,'tensor'=8] {'expert'}, dimensions={1} | all-to-all | bytes 491520 | tf_op jit(solution)/shard_map/all_to_all | solution.py:52
  35.6 0.8 pad_maximum_fusion.1
  36.4 0.0 all-gather.2.cloned.1.call-update
  36.4 35.5 %all-gather.2.cloned.1.call-done = bf16[3072,640]{0,1:T(8,128)(2,1)} async-done(((bf16[384,640]{0,1:T(8,128)(2,1)}), bf16[3072,640]{0,1:T(8,128)(2,1)}) %all-gather.2.cloned.1.call-update) | async-done | bytes 3932176 | tf_op jit(solution)/shard_map/all_gather | solution.py:55
  72.0 0.0 copy-start.3
  72.0 9.4 %fusion.2 = f32[320,2048]{1,0:T(8,128)S(1)} fusion(bf16[1,3072,2048]{2,1,0:T(8,128)(2,1)} %param.11, bf16[3072,640]{0,1:T(8,128)(2,1)} %all-gather.2.cloned.1.call-done), kind=kOutput, calls=%fused_computation.2 | convolution fusion | flops 4026531840 | bytes 17170432 | tf_op jit(solution)/shard_map/dot_general | solution.py:61
  81.4 0.0 copy-done.3
  81.4 8.8 %fusion.6 = f32[320,2048]{1,0:T(8,128)} fusion(bf16[1,3072,2048]{2,1,0:T(8,128)(2,1)} %param.12, bf16[3072,640]{0,1:T(8,128)(2,1)S(1)} %copy-done.3), kind=kOutput, calls=%fused_computation.6 | convolution fusion | flops 4026531840 | bytes 17170432 | tf_op jit(solution)/shard_map/dot_general | solution.py:64
  90.2 11.6 %multiply_reduce_fusion = (f32[320]{0:T(512)S(1)}, f32[320,2048]{1,0:T(8,128)}) fusion(f32[320,2048]{1,0:T(8,128)} %fusion.6, f32[320,2048]{1,0:T(8,128)S(1)} %fusion.2, bf16[1,2048,3072]{2,1,0:T(8,128)(2,1)} %param.13, bf16[3072,640]{0,1:T(8,128)(2,1)S(1)} %copy-done.3), kind=kOutput, calls=%fused_computation.14 | convolution fusion | flops 4031119104 | bytes 22414592 | tf_op jit(solution)/shard_map/dot_general | solution.py:65
  101.8 12.7 %fusion = f32[320,3072]{1,0:T(8,128)} fusion(bf16[1,3072,2048]{2,1,0:T(8,128)(2,1)} %param.11, f32[320,2048]{1,0:T(8,128)S(1)} %fusion.2, f32[320,2048]{1,0:T(8,128)} %get-tuple-element.7, f32[320,2048]{1,0:T(8,128)} %fusion.6), kind=kOutput, calls=%fused_computation | convolution fusion | flops 4033085440 | bytes 24379392 | tf_op jit(solution)/shard_map/dot_general | solution.py:72
  114.5 12.1 %fusion.16 = bf16[3072,320]{0,1:T(8,128)(2,1)} fusion(f32[320,3072]{1,0:T(8,128)} %fusion, bf16[1,3072,2048]{2,1,0:T(8,128)(2,1)} %param.12, f32[320,2048]{1,0:T(8,128)} %get-tuple-element.7, f32[320,2048]{1,0:T(8,128)S(1)} %fusion.2), kind=kOutput, calls=%fused_computation.13 | convolution fusion | flops 4032430080 | bytes 23724032 | tf_op jit(solution)/shard_map/dot_general | solution.py:73
  126.6 2.9 %copy.40 = bf16[3072,320]{1,0:T(8,128)(2,1)S(1)} copy(bf16[3072,320]{0,1:T(8,128)(2,1)} %fusion.16) | data formatting | bytes 3932160 | tf_op jit(solution)/shard_map/reshape | solution.py:85
  129.6 0.3 pad_maximum_fusion
  129.9 33.0 %all_to_all.39 = bf16[8,400,320]{2,1,0:T(8,128)(2,1)S(1)} all-to-all(bf16[8,400,320]{2,1,0:T(8,128)(2,1)S(1)} %pad_maximum_fusion), channel_id=1, replica_groups=mesh['expert'=4,'tensor'=8] {'tensor'}, dimensions={0} | all-to-all | bytes 4096000 | tf_op jit(solution)/shard_map/all_to_all | solution.py:87
  162.9 0.0 copy-start.1
  162.9 0.4 convert_reduce_fusion
  163.3 0.0 copy-start.2
  163.4 0.2 copy.39
  163.6 14.5 %all_to_all.40 = bf16[400,4,80]{0,2,1:T(8,128)(2,1)S(1)} all-to-all(bf16[400,4,80]{0,2,1:T(8,128)(2,1)S(1)} %bitcast.42), channel_id=1, replica_groups=mesh['expert'=4,'tensor'=8] {'expert'}, dimensions={1} | all-to-all | bytes 512000 | tf_op jit(solution)/shard_map/all_to_all | solution.py:105
  178.0 0.1 convert_element_type.115
  178.1 0.2 fusion.25
  178.4 0.1 broadcast_in_dim.57
  178.4 0.0 copy-done.2
  178.4 0.7 select_reduce_fusion
  179.2 1.2 convolution_convert_fusion.2
  180.3 0.0 copy-done.1
  (10 shorter events, 0.2 us)
Async XLA Ops:
  7.2 2.3 %copy-start = (bf16[384,128]{1,0:T(8,128)(2,1)S(1)}, bf16[384,128]{1,0:T(8,128)(2,1)}, u32[]{:S(2)}) copy-start(bf16[384,128]{1,0:T(8,128)(2,1)} %param.7) | copy-start | bytes 294916
  10.4 14.9 %all-to-all-start = ((bf16[384,4,80]{0,2,1:T(8,128)(2,1)}), bf16[384,4,80]{0,2,1:T(8,128)(2,1)S(1)}, u32[]{:S(2)}, u32[]{:S(2)}) async-start(bf16[384,4,80]{0,2,1:T(8,128)(2,1)} %bitcast.1), calls=%async_computation | async-start | bytes 491520 | tf_op jit(solution)/shard_map/all_to_all | solution.py:51
  16.7 55.2 %all-gather.2.cloned.1.call-start = ((), (), s32[]{:S(2)}) async-start(), calls=%async_computation.4 | async-start | bytes 4423680 | tf_op jit(solution)/shard_map/all_gather | solution.py:55
  72.0 9.4 %copy-start.3 = (bf16[3072,640]{0,1:T(8,128)(2,1)S(1)}, bf16[3072,640]{0,1:T(8,128)(2,1)}, u32[]{:S(2)}) copy-start(bf16[3072,640]{0,1:T(8,128)(2,1)} %all-gather.2.cloned.1.call-done) | copy-start | bytes 11796484
  162.9 17.5 %copy-start.1 = (bf16[384,128]{1,0:T(8,128)(2,1)S(1)}, bf16[384,128]{1,0:T(8,128)(2,1)}, u32[]{:S(2)}) copy-start(bf16[384,128]{1,0:T(8,128)(2,1)} %param.7) | copy-start | bytes 294916
  163.3 15.2 %copy-start.2 = (f32[128,2]{0,1:T(2,128)S(1)}, f32[128,2]{0,1:T(2,128)}, u32[]{:S(2)}) copy-start(f32[128,2]{0,1:T(2,128)} %param.10) | copy-start | bytes 3076
Sparse Core Ops, SparseCore 0:
  36.6 35.3 all-gather.1
